TPU v7x, 512 devices: a whole 4x8x8 slice. The times are simulated.
512 devices in a mesh: replica: 32 (over z_hi, x, core), tensor: 16 (over z_lo, y).
Axes of the slice: x: 4, y: 8, z: 8 (z_hi: 4, z_lo: 2; z = z_hi * 2 + z_lo), core: 2. Of those that a mesh axis runs over, the one named last changes fastest.
Arguments:
- weights: bfloat16 [32, 8192, 2048], P('replica', 'tensor'), may hold values from -6 to 6
- hidden: bfloat16 [32, 512, 8192], P('replica', None, 'tensor'), may hold values from -6 to 6
- out_grad: bfloat16 [32, 512, 2048], P('replica', None, 'tensor'), may hold values from -0.375 to 0.375
- factor_start: bfloat16 [2, 64, 8192], P(None, None, 'tensor'), may hold values from -6 to 6
- matching: int32 [2], replicated, may hold values from 1 to 31, as said below
Outputs:
- new_weights: bfloat16 [32, 8192, 2048], P('replica', 'tensor')
Inputs may be any that keep to these rules, and one draw needn't show every extreme that they name: In step t replica i is matched with replica i XOR matching[t]; in one of the steps matching equals 31.
All inputs are finite; a program needn't handle non-finite values.
Results may differ from a plain program's by a relative error of at most 0.014.
Values may be sent and summed in bfloat16 or wider, within the bound.
A program may use at most 64 MiB of HBM per device.

v0:
```python
import jax
import jax.numpy as jnp
from jax import lax
from jax.sharding import PartitionSpec as P

STEPS = 2
TOK = 256


learn_rate = 0.1
momentum_decay = 0.9


def from_partner(value, axis, bit):
    mask = 2**bit
    pairs = [(source, source ^ mask) for source in range(lax.axis_size(axis))]
    return lax.ppermute(value, axis, pairs)


def swap_left_side(payload, pairing):
    for bit_number in range(lax.axis_size("replica").bit_length() - 1):
        arrived = from_partner(payload.astype(jnp.bfloat16), "replica", bit_number).astype(
            payload.dtype
        )
        chosen = pairing // 2**bit_number % 2
        payload = jnp.where(chosen == 1, arrived, payload)
    return payload


def swap_right_side(payload, pairing):
    for bit_number in range(lax.axis_size("replica").bit_length() - 1):
        arrived = from_partner(payload.astype(jnp.bfloat16), "replica", bit_number).astype(
            payload.dtype
        )
        chosen = pairing // 2**bit_number % 2
        payload = jnp.where(chosen == 1, arrived, payload)
    return payload


def orthonormal(gram_matrix, difference):
    lower_factor = jnp.linalg.cholesky(gram_matrix)
    return lax.linalg.triangular_solve(lower_factor, difference, left_side=True, lower=True)


def per_device(weights, hidden, out_grad, factor_start, matching):
    current = weights[0]
    hidden_all = hidden[0]
    grads_all = out_grad[0]
    momentum = None
    for step_index in range(STEPS):
        hidden_step = hidden_all[step_index * TOK : (step_index + 1) * TOK]
        grads_step = grads_all[step_index * TOK : (step_index + 1) * TOK]
        gradient = lax.dot_general(
            hidden_step,
            lax.all_gather(grads_step, "tensor", axis=1, tiled=True),
            (((0,), (0,)), ((), ())),
            preferred_element_type=jnp.float32,
        )
        if momentum is None:
            momentum = gradient
        else:
            momentum = momentum_decay * momentum + gradient
        updated = (current.astype(jnp.float32) - learn_rate * momentum).astype(jnp.bfloat16)
        start_factor = factor_start[step_index]
        pairing = matching[step_index]
        local_left = jnp.dot(start_factor, updated, preferred_element_type=jnp.float32)
        left_total = lax.psum(local_left.astype(jnp.bfloat16), "tensor").astype(jnp.float32)
        left_diff = left_total - swap_left_side(left_total, pairing)
        gram_matrix = jnp.dot(left_diff, left_diff.T, precision=lax.Precision.HIGHEST)
        ortho_bf = orthonormal(gram_matrix, left_diff).astype(jnp.bfloat16)
        right_prod = lax.dot_general(
            ortho_bf, updated, (((1,), (1,)), ((), ())), preferred_element_type=jnp.float32
        )
        right_diff = (right_prod - swap_right_side(right_prod, pairing)).astype(jnp.bfloat16)
        change = lax.dot_general(
            right_diff, ortho_bf, (((0,), (0,)), ((), ())), preferred_element_type=jnp.float32
        )
        current = (updated.astype(jnp.float32) - 0.5 * change).astype(jnp.bfloat16)
    return current[None]


def solution(mesh):
    return jax.shard_map(
        per_device,
        mesh=mesh,
        in_specs=(
            P("replica", "tensor", None),
            P("replica", None, "tensor"),
            P("replica", None, "tensor"),
            P(None, None, "tensor"),
            P(),
        ),
        out_specs=P("replica", "tensor", None),
        check_vma=False,
    )
```

profile of v0, /device:TPU:1, one launch (start us, length us, event | category | flops | bytes accessed | tf_op | source)
XLA Modules:
  0.0 608.6 jit_solution(4303850589164931657)
XLA Ops:
  8.3 63.2 %all-gather.5.cloned.1.call-done = bf16[1,256,2048]{2,1,0:T(8,128)(2,1)} async-done(((bf16[1,256,128]{2,1,0:T(8,128)(2,1)}), bf16[1,256,2048]{2,1,0:T(8,128)(2,1)}) %all-gather.5.cloned.1.call-update) | async-done | bytes 1048592 | tf_op jit(solution)/shard_map/all_gather | solution.py:55
  77.0 140.0 %all-reduce.3.cloned.1.call-done = bf16[64,2048]{1,0:T(8,128)(2,1)} async-done(((bf16[64,2048]{1,0:T(8,128)(2,1)}), bf16[64,2048]{1,0:T(8,128)(2,1)}) %all-reduce.3.cloned.1.call-update) | async-done | bytes 262160 | tf_op jit(solution)/shard_map/psum | solution.py:67
  217.1 12.7 %collective-permute-start = (bf16[64,2048]{1,0:T(8,128)(2,1)}, bf16[64,2048]{1,0:T(8,128)(2,1)S(1)}, u32[]{:S(2)}, u32[]{:S(2)}) collective-permute-start(bf16[64,2048]{1,0:T(8,128)(2,1)} %all-reduce.3.cloned.1.call-done), channel_id=1, source_target_pairs={{0,16},{16,0},{32,48},{48,32},{64,80},{80,64},{96,112},{112,96},{1... | collective-permute-start | bytes 786440 | tf_op jit(solution)/shard_map/ppermute | solution.py:17
  237.1 6.0 collective-permute-done.1
  244.2 4.6 collective-permute-start.2
  248.9 5.8 collective-permute-done.2
  260.3 12.2 %collective-permute-done.3 = bf16[64,2048]{1,0:T(8,128)(2,1)} collective-permute-done((bf16[64,2048]{1,0:T(8,128)(2,1)S(1)}, bf16[64,2048]{1,0:T(8,128)(2,1)}, u32[]{:S(2)}, u32[]{:S(2)}) %collective-permute-start.3) | collective-permute-done | bytes 262176 | tf_op jit(solution)/shard_map/ppermute | solution.py:17
  274.5 6.1 %collective-permute-start.4 = (bf16[64,2048]{1,0:T(8,128)(2,1)}, bf16[64,2048]{1,0:T(8,128)(2,1)S(1)}, u32[]{:S(2)}, u32[]{:S(2)}) collective-permute-start(bf16[64,2048]{1,0:T(8,128)(2,1)} %get-tuple-element.13), channel_id=1, source_target_pairs={{0,256},{16,272},{32,288},{48,304},{64,320},{80,336},{96,352},{112... | collective-permute-start | bytes 786440 | tf_op jit(solution)/shard_map/ppermute | solution.py:17
  280.7 12.8 %collective-permute-done.4 = bf16[64,2048]{1,0:T(8,128)(2,1)S(1)} collective-permute-done((bf16[64,2048]{1,0:T(8,128)(2,1)}, bf16[64,2048]{1,0:T(8,128)(2,1)S(1)}, u32[]{:S(2)}, u32[]{:S(2)}) %collective-permute-start.4) | collective-permute-done | bytes 262176 | tf_op jit(solution)/shard_map/ppermute | solution.py:17
  294.2 5.8 cholesky.44
  301.4 5.5 custom-call.6
  321.0 4.6 collective-permute-start.7
  347.5 131.4 %all-reduce.5.cloned.1.call-done = bf16[64,2048]{1,0:T(8,128)(2,1)} async-done(((bf16[64,2048]{1,0:T(8,128)(2,1)}), bf16[64,2048]{1,0:T(8,128)(2,1)}) %all-reduce.5.cloned.1.call-update) | async-done | bytes 262160 | tf_op jit(solution)/shard_map/psum | solution.py:67
  478.9 12.7 %collective-permute-start.10 = (bf16[64,2048]{1,0:T(8,128)(2,1)}, bf16[64,2048]{1,0:T(8,128)(2,1)S(1)}, u32[]{:S(2)}, u32[]{:S(2)}) collective-permute-start(bf16[64,2048]{1,0:T(8,128)(2,1)} %all-reduce.5.cloned.1.call-done), channel_id=1, source_target_pairs={{0,16},{16,0},{32,48},{48,32},{64,80},{80,64},{96,112},{112,96},{1... | collective-permute-start | bytes 786440 | tf_op jit(solution)/shard_map/ppermute | solution.py:17
  498.3 6.0 collective-permute-done.11
  505.4 4.6 collective-permute-start.12
  510.0 5.8 collective-permute-done.12
  521.4 12.2 %collective-permute-done.13 = bf16[64,2048]{1,0:T(8,128)(2,1)} collective-permute-done((bf16[64,2048]{1,0:T(8,128)(2,1)S(1)}, bf16[64,2048]{1,0:T(8,128)(2,1)}, u32[]{:S(2)}, u32[]{:S(2)}) %collective-permute-start.13) | collective-permute-done | bytes 262176 | tf_op jit(solution)/shard_map/ppermute | solution.py:17
  535.6 6.3 %collective-permute-start.14 = (bf16[64,2048]{1,0:T(8,128)(2,1)}, bf16[64,2048]{1,0:T(8,128)(2,1)S(1)}, u32[]{:S(2)}, u32[]{:S(2)}) collective-permute-start(bf16[64,2048]{1,0:T(8,128)(2,1)} %get-tuple-element.9), channel_id=1, source_target_pairs={{0,256},{16,272},{32,288},{48,304},{64,320},{80,336},{96,352},{112... | collective-permute-start | bytes 786440 | tf_op jit(solution)/shard_map/ppermute | solution.py:17
  542.0 12.6 %collective-permute-done.14 = bf16[64,2048]{1,0:T(8,128)(2,1)S(1)} collective-permute-done((bf16[64,2048]{1,0:T(8,128)(2,1)}, bf16[64,2048]{1,0:T(8,128)(2,1)S(1)}, u32[]{:S(2)}, u32[]{:S(2)}) %collective-permute-start.14) | collective-permute-done | bytes 262176 | tf_op jit(solution)/shard_map/ppermute | solution.py:17
  555.4 5.8 cholesky.55
  562.5 4.9 custom-call.7
  578.1 4.6 collective-permute-start.17
  594.6 5.4 collective-permute-done.19
  (92 shorter events, 97.8 us)
Async XLA Ops:
  6.5 65.0 %all-gather.5.cloned.1.call-start = ((), (), s32[]{:S(2)}) async-start(), calls=%async_computation.2 | async-start | bytes 1114112 | tf_op jit(solution)/shard_map/all_gather | solution.py:55
  8.3 208.8 %all-reduce.3.cloned.1.call-start = ((), (), s32[]{:S(2)}) async-start(), calls=%async_computation | async-start | bytes 524288 | tf_op jit(solution)/shard_map/psum | solution.py:67
  77.0 260.1 %all-gather.7.cloned.1.call-start = ((), (), s32[]{:S(2)}) async-start(), calls=%async_computation.3 | async-start | bytes 1114112 | tf_op jit(solution)/shard_map/all_gather | solution.py:55
  217.1 15.2 %collective-permute-start = (bf16[64,2048]{1,0:T(8,128)(2,1)}, bf16[64,2048]{1,0:T(8,128)(2,1)S(1)}, u32[]{:S(2)}, u32[]{:S(2)}) collective-permute-start(bf16[64,2048]{1,0:T(8,128)(2,1)} %all-reduce.3.cloned.1.call-done), channel_id=1, source_target_pairs={{0,16},{16,0},{32,48},{48,32},{64,80},{80,64},{96,112},{112,96},{1... | collective-permute-start | bytes 786440 | tf_op jit(solution)/shard_map/ppermute | solution.py:17
  233.4 9.8 %collective-permute-start.1 = (bf16[64,2048]{1,0:T(8,128)(2,1)S(1)}, bf16[64,2048]{1,0:T(8,128)(2,1)S(1)}, u32[]{:S(2)}, u32[]{:S(2)}) collective-permute-start(bf16[64,2048]{1,0:T(8,128)(2,1)S(1)} %fusion.8), channel_id=1, source_target_pairs={{0,32},{16,48},{32,0},{48,16},{64,96},{80,112},{96,64},{112,80},{1... | collective-permute-start | bytes 786440 | tf_op jit(solution)/shard_map/ppermute | solution.py:17
  244.2 10.4 %collective-permute-start.2 = (bf16[64,2048]{1,0:T(8,128)(2,1)S(1)}, bf16[64,2048]{1,0:T(8,128)(2,1)S(1)}, u32[]{:S(2)}, u32[]{:S(2)}) collective-permute-start(bf16[64,2048]{1,0:T(8,128)(2,1)S(1)} %fusion.18), channel_id=1, source_target_pairs={{0,64},{16,80},{32,96},{48,112},{64,0},{80,16},{96,32},{112,48},{1... | collective-permute-start | bytes 786440 | tf_op jit(solution)/shard_map/ppermute | solution.py:17
  255.8 16.7 %collective-permute-start.3 = (bf16[64,2048]{1,0:T(8,128)(2,1)S(1)}, bf16[64,2048]{1,0:T(8,128)(2,1)}, u32[]{:S(2)}, u32[]{:S(2)}) collective-permute-start(bf16[64,2048]{1,0:T(8,128)(2,1)S(1)} %fusion.10), channel_id=1, source_target_pairs={{0,128},{16,144},{32,160},{48,176},{64,192},{80,208},{96,224},{112... | collective-permute-start | bytes 786440 | tf_op jit(solution)/shard_map/ppermute | solution.py:17
  274.5 19.0 %collective-permute-start.4 = (bf16[64,2048]{1,0:T(8,128)(2,1)}, bf16[64,2048]{1,0:T(8,128)(2,1)S(1)}, u32[]{:S(2)}, u32[]{:S(2)}) collective-permute-start(bf16[64,2048]{1,0:T(8,128)(2,1)} %get-tuple-element.13), channel_id=1, source_target_pairs={{0,256},{16,272},{32,288},{48,304},{64,320},{80,336},{96,352},{112... | collective-permute-start | bytes 786440 | tf_op jit(solution)/shard_map/ppermute | solution.py:17
  280.7 198.2 %all-reduce.5.cloned.1.call-start = ((), (), s32[]{:S(2)}) async-start(), calls=%async_computation.1 | async-start | bytes 524288 | tf_op jit(solution)/shard_map/psum | solution.py:67
  311.3 4.2 collective-permute-start.5
  315.5 5.4 collective-permute-start.6
  321.0 6.5 %collective-permute-start.7 = (bf16[64,512]{1,0:T(8,128)(2,1)S(1)}, bf16[64,512]{1,0:T(8,128)(2,1)S(1)}, u32[]{:S(2)}, u32[]{:S(2)}) collective-permute-start(bf16[64,512]{1,0:T(8,128)(2,1)S(1)} %get-tuple-element.11), channel_id=1, source_target_pairs={{0,64},{16,80},{32,96},{48,112},{64,0},{80,16},{96,32},{112,48},{1... | collective-permute-start | bytes 196616 | tf_op jit(solution)/shard_map/ppermute | solution.py:17
  327.5 6.0 collective-permute-start.8
  333.5 9.7 %collective-permute-start.9 = (bf16[64,512]{1,0:T(8,128)(2,1)S(1)}, bf16[64,512]{1,0:T(8,128)(2,1)S(1)}, u32[]{:S(2)}, u32[]{:S(2)}) collective-permute-start(bf16[64,512]{1,0:T(8,128)(2,1)S(1)} %fusion.30), channel_id=1, source_target_pairs={{0,256},{16,272},{32,288},{48,304},{64,320},{80,336},{96,352},{112... | collective-permute-start | bytes 196616 | tf_op jit(solution)/shard_map/ppermute | solution.py:17
  478.9 14.6 %collective-permute-start.10 = (bf16[64,2048]{1,0:T(8,128)(2,1)}, bf16[64,2048]{1,0:T(8,128)(2,1)S(1)}, u32[]{:S(2)}, u32[]{:S(2)}) collective-permute-start(bf16[64,2048]{1,0:T(8,128)(2,1)} %all-reduce.5.cloned.1.call-done), channel_id=1, source_target_pairs={{0,16},{16,0},{32,48},{48,32},{64,80},{80,64},{96,112},{112,96},{1... | collective-permute-start | bytes 786440 | tf_op jit(solution)/shard_map/ppermute | solution.py:17
  494.5 9.8 %collective-permute-start.11 = (bf16[64,2048]{1,0:T(8,128)(2,1)S(1)}, bf16[64,2048]{1,0:T(8,128)(2,1)S(1)}, u32[]{:S(2)}, u32[]{:S(2)}) collective-permute-start(bf16[64,2048]{1,0:T(8,128)(2,1)S(1)} %fusion.9), channel_id=1, source_target_pairs={{0,32},{16,48},{32,0},{48,16},{64,96},{80,112},{96,64},{112,80},{1... | collective-permute-start | bytes 786440 | tf_op jit(solution)/shard_map/ppermute | solution.py:17
  505.4 10.4 %collective-permute-start.12 = (bf16[64,2048]{1,0:T(8,128)(2,1)S(1)}, bf16[64,2048]{1,0:T(8,128)(2,1)S(1)}, u32[]{:S(2)}, u32[]{:S(2)}) collective-permute-start(bf16[64,2048]{1,0:T(8,128)(2,1)S(1)} %fusion.19), channel_id=1, source_target_pairs={{0,64},{16,80},{32,96},{48,112},{64,0},{80,16},{96,32},{112,48},{1... | collective-permute-start | bytes 786440 | tf_op jit(solution)/shard_map/ppermute | solution.py:17
  517.0 16.7 %collective-permute-start.13 = (bf16[64,2048]{1,0:T(8,128)(2,1)S(1)}, bf16[64,2048]{1,0:T(8,128)(2,1)}, u32[]{:S(2)}, u32[]{:S(2)}) collective-permute-start(bf16[64,2048]{1,0:T(8,128)(2,1)S(1)} %fusion.11), channel_id=1, source_target_pairs={{0,128},{16,144},{32,160},{48,176},{64,192},{80,208},{96,224},{112... | collective-permute-start | bytes 786440 | tf_op jit(solution)/shard_map/ppermute | solution.py:17
  535.6 19.0 %collective-permute-start.14 = (bf16[64,2048]{1,0:T(8,128)(2,1)}, bf16[64,2048]{1,0:T(8,128)(2,1)S(1)}, u32[]{:S(2)}, u32[]{:S(2)}) collective-permute-start(bf16[64,2048]{1,0:T(8,128)(2,1)} %get-tuple-element.9), channel_id=1, source_target_pairs={{0,256},{16,272},{32,288},{48,304},{64,320},{80,336},{96,352},{112... | collective-permute-start | bytes 786440 | tf_op jit(solution)/shard_map/ppermute | solution.py:17
  568.8 4.2 collective-permute-start.15
  573.0 5.0 collective-permute-start.16
  578.1 6.5 %collective-permute-start.17 = (bf16[64,512]{1,0:T(8,128)(2,1)S(1)}, bf16[64,512]{1,0:T(8,128)(2,1)S(1)}, u32[]{:S(2)}, u32[]{:S(2)}) collective-permute-start(bf16[64,512]{1,0:T(8,128)(2,1)S(1)} %get-tuple-element.6), channel_id=1, source_target_pairs={{0,64},{16,80},{32,96},{48,112},{64,0},{80,16},{96,32},{112,48},{1... | collective-permute-start | bytes 196616 | tf_op jit(solution)/shard_map/ppermute | solution.py:17
  584.6 5.9 collective-permute-start.18
  590.5 9.5 %collective-permute-start.19 = (bf16[64,512]{1,0:T(8,128)(2,1)S(1)}, bf16[64,512]{1,0:T(8,128)(2,1)S(1)}, u32[]{:S(2)}, u32[]{:S(2)}) collective-permute-start(bf16[64,512]{1,0:T(8,128)(2,1)S(1)} %fusion.31), channel_id=1, source_target_pairs={{0,256},{16,272},{32,288},{48,304},{64,320},{80,336},{96,352},{112... | collective-permute-start | bytes 196616 | tf_op jit(solution)/shard_map/ppermute | solution.py:17
  (10 other events, 492.4 us)
Sparse Core Ops, SparseCore 0:
  9.4 62.0 all-gather.4
  77.1 139.9 all-reduce.2
  280.8 51.7 all-gather.6
  347.6 131.2 all-reduce.4
where the time goes:
time: 613 us; the launch traced here: 609 us
  waiting for transfers between devices  435 us (71%)
  starting transfers between devices  95.5 us (16%)
  other arithmetic  35.4 us (6%)
  between operations  19 us (3%)
  matrix products  18.9 us (3%)
    psum x2, waiting for transfers between devices, per_device(): lax.psum(local_left.astype(jnp.bfloat16), 'tensor').astype(jnp.float32)  271 us
    ppermute x20, waiting for transfers between devices, from_partner(): return lax.ppermute(value, axis, pairs)  101 us
    ppermute x20, starting transfers between devices, from_partner(): return lax.ppermute(value, axis, pairs)  95.4 us
    all_gather x2, waiting for transfers between devices, per_device(): lax.all_gather(grads_step, 'tensor', axis=1, tiled=True)  63.2 us
    another operation x6, other arithmetic, orthonormal(): lower_factor = jnp.linalg.cholesky(gram_matrix)  13 us
  transfers between devices with their start and end apart: 24, of which 21 were waited for; matrix products, arithmetic and copies ran while one was open for 3% of the time, Pallas kernels for 0%

commit v1 on v0

v1 whole, which is shorter than its diff:
```python
import functools

import jax
import jax.numpy as jnp
from jax import lax
from jax.experimental import pallas as pl
from jax.experimental.pallas import tpu as pltpu
from jax.sharding import PartitionSpec as P

F32 = jnp.float32
BF = jnp.bfloat16
MESH = pl.DeviceIdType.MESH
RANK = 64
TOK = 256
Y = 8
OFFSETS = [(4, 0), (3, 0), (5, 0), (2, 0), (6, 0), (4, 1), (3, 1), (5, 1), (2, 1), (6, 1), (1, 0), (7, 0), (1, 1), (7, 1), (0, 1)]
CORE_MASKS = [1]
X_MASKS = [2, 4, 6]
Z_MASKS = [8, 16, 24]


def flip(index, mask):
    for bit in range(5):
        if mask >> bit & 1:
            index = index + (1 - 2 * lax.rem(lax.div(index, 2**bit), 2)) * 2**bit
    return index


def nn(a, b):
    return lax.dot_general(a, b, (((1,), (0,)), ((), ())), preferred_element_type=F32)


def nt(a, b):
    return lax.dot_general(a, b, (((1,), (1,)), ((), ())), preferred_element_type=F32)


def tn(a, b):
    return lax.dot_general(a, b, (((0,), (0,)), ((), ())), preferred_element_type=F32)


def inverse_lower_factor(gram):
    n = RANK
    row_at = lax.broadcasted_iota(jnp.int32, (n, n), 0)
    col_at = lax.broadcasted_iota(jnp.int32, (n, n), 1)
    eye = (row_at == col_at).astype(F32)
    wide = jnp.concatenate([gram, eye], axis=1)
    rows = [wide[8 * j : 8 * j + 8] for j in range(8)]
    sub = lax.broadcasted_iota(jnp.int32, (8, 128), 0)

    def spread(block, s):
        return jnp.broadcast_to(block[s : s + 1, :], (8, 128))

    for jb in range(8):
        cols = [
            [jnp.broadcast_to(rows[j][:, 8 * jb + q : 8 * jb + q + 1], (8, 128)) if j >= jb else None for j in range(8)]
            for q in range(8)
        ]
        for s in range(8):
            pivot_row = spread(rows[jb], s)
            inverse = 1.0 / spread(cols[s][jb], s)
            ahead = [spread(cols[q][jb], s) if q > s else None for q in range(8)]
            for j in range(jb, 8):
                factor = cols[s][j] * inverse
                if j == jb:
                    factor = jnp.where(sub > s, factor, 0.0)
                rows[j] = rows[j] - factor * pivot_row
                for q in range(s + 1, 8):
                    cols[q][j] = cols[q][j] - factor * ahead[q]
    wide = jnp.concatenate(rows, axis=0)
    pivots = jnp.sum(wide[:, :n] * eye, axis=1, keepdims=True)
    return wide[:, n:] * lax.rsqrt(pivots)


def orthonormal(diff):
    inverse = inverse_lower_factor(nt(diff, diff))
    high = inverse.astype(BF)
    low = (inverse - high.astype(F32)).astype(BF)
    return nn(jnp.concatenate([high, low], axis=1), jnp.concatenate([diff, diff], axis=0)).astype(BF)


class Sends:
    def __init__(self, send_sems, recv_sems):
        self.send_sems, self.recv_sems = send_sems, recv_sems
        self.count = 0
        self.open = []

    def start(self, copies, total):
        number = self.count
        self.count += 1
        for source, target, device in copies:
            pltpu.make_async_remote_copy(
                src_ref=source,
                dst_ref=target,
                send_sem=self.send_sems.at[number],
                recv_sem=self.recv_sems.at[number],
                device_id=device,
                device_id_type=MESH,
            ).start()
        self.open.append((number, total))
        return number, total

    def wait(self, ticket):
        number, total = ticket
        pltpu.make_async_copy(total, total, self.recv_sems.at[number]).wait()

    def finish(self):
        for number, total in self.open:
            pltpu.make_async_copy(total, total, self.send_sems.at[number]).wait()


class Exchange:
    def __init__(self, sends, replica, tensor, mask, static, bufs):
        self.sends, self.replica, self.tensor = sends, replica, tensor
        self.mask, self.static = mask, static
        self.core, self.xs, self.zs = bufs
        self.ticket = None

    def _send(self, buf, masks):
        copies = [
            (buf.at[0], buf.at[k + 1], (flip(self.replica, mask), self.tensor)) for k, mask in enumerate(masks)
        ]
        self.ticket = self.sends.start(copies, buf.at[pl.ds(1, len(masks))])

    def begin(self, payload):
        self.core[0] = payload
        if self.static is not None:
            self._send(self.core, [self.static])
        else:
            self._send(self.core, CORE_MASKS)

    def along_x(self):
        if self.static is None:
            self.sends.wait(self.ticket)
            self.xs[0] = self.core[lax.rem(self.mask, 2)]
            self._send(self.xs, X_MASKS)

    def along_z(self):
        if self.static is None:
            self.sends.wait(self.ticket)
            self.zs[0] = self.xs[lax.rem(lax.div(self.mask, 2), 4)]
            self._send(self.zs, Z_MASKS)

    def end(self):
        self.sends.wait(self.ticket)
        if self.static is not None:
            return self.core[1]
        return self.zs[lax.rem(lax.div(self.mask, 8), 4)]


def kernel(
    static, m_ref, w_hbm, h_hbm, g_hbm, s_hbm, o_hbm,
    w, h, s, gown, gf, tsend, trecv0, trecv1, tf, zsend, zrecv0, zrecv1, block,
    c0, x0, z0, df0, ef, o0, cl, xl, zl, df1, o1, cr0, xr0, zr0, cr1, xr1, zr1,
    rd0, v, out, send_sems, recv_sems, load_sems, store_sems,
):
    replica = lax.axis_index("replica")
    tensor = lax.axis_index("tensor")
    y = lax.rem(tensor, Y)
    z = lax.div(tensor, Y)

    def at(dy, dz):
        return lax.rem(y + dy + Y, Y) + (z if dz == 0 else 1 - z) * Y

    peers = [(replica, at(dy, dz)) for dy, dz in OFFSETS]
    masks = []
    if None in static:
        masks = CORE_MASKS + X_MASKS + Z_MASKS
    masks = masks + [m for m in set(static) if m is not None]

    barrier = pltpu.get_barrier_semaphore()
    for device in peers + [(flip(replica, mask), tensor) for mask in masks]:
        pl.semaphore_signal(barrier, inc=1, device_id=device, device_id_type=MESH)

    mine = pl.ds(pl.multiple_of(tensor * 128, 128), 128)

    loads = [
        pltpu.make_async_copy(s_hbm, s, load_sems.at[0]),
        pltpu.make_async_copy(h_hbm.at[0], h, load_sems.at[1]),
        pltpu.make_async_copy(w_hbm.at[0], w, load_sems.at[2]),
        pltpu.make_async_copy(g_hbm.at[0], gown, load_sems.at[3]),
        pltpu.make_async_copy(g_hbm.at[0], gf.at[:, mine], load_sems.at[4]),
    ]
    for load in loads:
        load.start()
    loads[0].wait()
    loads[1].wait()
    tsend[...] = nt(h[...], s[...]).astype(BF)
    loads[2].wait()

    def starting_left(i, carry):
        cut = pl.ds(pl.multiple_of(i * 512, 512), 512)
        zsend[:, cut] = nn(s[...], w[:, cut]).astype(BF)
        return carry

    lax.fori_loop(0, 4, starting_left, 0)
    loads[3].wait()
    loads[4].wait()

    pl.semaphore_wait(barrier, len(peers) + len(masks))

    sends = Sends(send_sems, recv_sems)

    def scatter_tokens(step, into):
        copies = []
        for k, (r, t) in enumerate(peers):
            rows = pl.ds(pl.multiple_of(t * 16 + step * TOK, 16), 16)
            copies.append((tsend.at[rows], into.at[k], (r, t)))
        return sends.start(copies, into)

    def scatter_columns(step, into):
        copies = []
        for k, (r, t) in enumerate(peers):
            cut = pl.ds(pl.multiple_of(t * 128, 128), 128)
            copies.append((zsend.at[pl.ds(step * RANK, RANK), cut], into.at[k], (r, t)))
        return sends.start(copies, into)

    def gather_columns(source, into):
        return sends.start([(source, into.at[:, mine], p) for p in peers], into.at[:, pl.ds(0, 15 * 128)])

    def sum_tokens(step, arrived):
        rows = pl.ds(pl.multiple_of(tensor * 16 + step * TOK, 16), 16)
        total = tsend[rows].astype(F32)
        for k in range(15):
            total = total + arrived[k].astype(F32)
        tf[rows] = total.astype(BF)
        return sends.start([(tf.at[rows], tf.at[rows], p) for p in peers], tf.at[pl.ds(0, 15 * 16)])

    def sum_columns(step, arrived):
        total = zsend[pl.ds(step * RANK, RANK), mine].astype(F32)
        for k in range(15):
            total = total + arrived[k].astype(F32)
        return total

    gshard = gown

    def forward(dy_from, dz, dy_to):
        cut = pl.ds(pl.multiple_of(at(dy_from, dz) * 128, 128), 128)
        source = gown if (dy_from, dz) == (0, 0) else gf.at[:, cut]
        return sends.start([(source, gf.at[:, cut], (replica, at(dy_to, 0)))], gshard)

    t0 = scatter_tokens(0, trecv0)
    q0 = scatter_columns(0, zrecv0)
    t1 = scatter_tokens(1, trecv1)
    q1 = scatter_columns(1, zrecv1)
    gz = sends.start([(gown, gf.at[:, mine], (replica, at(0, 1)))], gshard)
    ra = forward(0, 0, 1)
    la = forward(0, 0, -1)

    sends.wait(t0)
    t0 = sum_tokens(0, trecv0)
    sends.wait(t1)
    t1 = sum_tokens(1, trecv1)
    sends.wait(q0)
    left0 = sum_columns(0, zrecv0)
    sends.wait(q1)
    left1 = sum_columns(1, zrecv1)
    sends.wait(t0)
    grad0 = tn(tf[pl.ds(0, TOK)], gown[pl.ds(0, TOK)])
    y0 = (left0 - 0.1 * grad0[:RANK]).astype(BF)
    x1 = left1 - 0.1 * grad0[RANK:]

    first = Exchange(sends, replica, tensor, m_ref[0], static[0], (c0, x0, z0))
    first.begin(jnp.concatenate([y0, x1.astype(BF)], axis=0))
    sends.wait(gz)
    rb = forward(0, 1, 1)
    lb = forward(0, 1, -1)
    first.along_x()
    sends.wait(ra)
    ra = forward(-1, 0, 1)
    sends.wait(la)
    la = forward(1, 0, -1)
    sends.wait(t1)
    grad1 = tn(tf[pl.ds(TOK, TOK)], gown[pl.ds(TOK, TOK)])
    y1 = x1 - 0.09 * grad0[RANK:] - 0.1 * grad1[RANK:]
    first.along_z()
    sends.wait(rb)
    rb = forward(-1, 1, 1)
    sends.wait(lb)
    lb = forward(1, 1, -1)
    other = first.end()
    diff = (y0.astype(F32) - other[:RANK].astype(F32)).astype(BF)
    both = (x1 + other[RANK:].astype(F32)).astype(BF)
    block[0] = diff
    block[1] = both
    df0[:, mine] = diff
    ef[:, mine] = both
    d0 = gather_columns(block.at[0], df0)
    e0 = gather_columns(block.at[1], ef)
    sends.wait(ra)
    ra = forward(-2, 0, 1)
    sends.wait(la)
    la = forward(2, 0, -1)
    sends.wait(d0)
    o0[...] = orthonormal(df0[...])
    sends.wait(e0)
    moved = nt(ef[...], o0[...]).astype(BF)
    l1 = (y1 - 0.5 * nn(moved, o0[:, mine])).astype(BF)

    second = Exchange(sends, replica, tensor, m_ref[1], static[1], (cl, xl, zl))
    second.begin(l1)
    sends.wait(rb)
    rb = forward(-2, 1, 1)
    sends.wait(lb)
    lb = forward(2, 1, -1)
    second.along_x()
    sends.wait(ra)
    ra = forward(-3, 0, 1)
    sends.wait(la)
    sends.wait(rb)
    sends.wait(lb)
    lb = forward(3, 1, -1)
    second.along_z()
    sends.wait(ra)
    sends.wait(lb)
    r0 = nt(o0[...], w[...]) - 0.1 * nn(nt(o0[...], gf[pl.ds(0, TOK)]).astype(BF), h[pl.ds(0, TOK)])
    r0 = r0.astype(BF)
    right0 = Exchange(sends, replica, tensor, m_ref[0], static[0], (cr0, xr0, zr0))
    right0.begin(r0)
    diff = (l1.astype(F32) - second.end().astype(F32)).astype(BF)
    block[2] = diff
    df1[:, mine] = diff
    d1 = gather_columns(block.at[2], df1)
    right0.along_x()
    right0.along_z()

    def settled(i, carry):
        cut = pl.ds(pl.multiple_of(i * 256, 256), 256)
        early = tn(h[pl.ds(0, TOK)], gf[pl.ds(0, TOK), cut])
        late = tn(h[pl.ds(TOK, TOK)], gf[pl.ds(TOK, TOK), cut])
        v[:, cut] = w[:, cut].astype(F32) - 0.19 * early - 0.1 * late
        return carry

    sends.wait(d1)
    o1[...] = orthonormal(df1[...])
    grad_part = nt(o1[...], gf[...])
    grad_part = jnp.concatenate([0.19 * grad_part[:, :TOK], 0.1 * grad_part[:, TOK:]], axis=1).astype(BF)
    cross = (0.5 * nt(o1[...], o0[...])).astype(BF)
    r1 = nt(o1[...], w[...]) - nn(grad_part, h[...])
    diff0 = (r0.astype(F32) - right0.end().astype(F32)).astype(BF)
    rd0[...] = diff0
    r1 = (r1 - nn(cross, diff0)).astype(BF)
    right1 = Exchange(sends, replica, tensor, m_ref[1], static[1], (cr1, xr1, zr1))
    right1.begin(r1)
    right1.along_x()
    lax.fori_loop(0, 4, settled, 0)
    right1.along_z()
    lax.fori_loop(4, 8, settled, 0)

    def first_move(i, carry):
        cut = pl.ds(pl.multiple_of(i * 256, 256), 256)
        v[:, cut] = v[:, cut] - 0.5 * tn(rd0[...], o0[:, cut])
        return carry

    lax.fori_loop(0, 8, first_move, 0)
    diff1 = (r1.astype(F32) - right1.end().astype(F32)).astype(BF)
    stores = []
    for i in range(4):
        rows = pl.ds(128 * i, 128)
        out[rows] = (v[rows] - 0.5 * tn(diff1[:, 128 * i : 128 * i + 128], o1[...])).astype(BF)
        store = pltpu.make_async_copy(out.at[rows], o_hbm.at[0, rows], store_sems.at[i])
        store.start()
        stores.append(store)
    sends.finish()
    for store in stores:
        store.wait()


def steps(static, number, matching, weights, hidden, out_grad, factors):
    def bf(*shape):
        return pltpu.VMEM(shape, BF)

    anywhere = pl.BlockSpec(memory_space=pl.ANY)
    return pl.pallas_call(
        functools.partial(kernel, static),
        out_shape=jax.ShapeDtypeStruct(weights.shape, BF),
        in_specs=[pl.BlockSpec(memory_space=pltpu.SMEM)] + [anywhere] * 4,
        out_specs=anywhere,
        scratch_shapes=[
            bf(512, 2048), bf(512, 512), bf(128, 512), bf(512, 128), bf(512, 2048),
            bf(512, 128), bf(15, 16, 128), bf(15, 16, 128), bf(512, 128),
            bf(128, 2048), bf(15, 64, 128), bf(15, 64, 128), bf(3, 64, 128),
            bf(2, 128, 128), bf(4, 128, 128), bf(4, 128, 128), bf(64, 2048), bf(64, 2048), bf(64, 2048),
            bf(2, 64, 128), bf(4, 64, 128), bf(4, 64, 128), bf(64, 2048), bf(64, 2048),
            bf(2, 64, 512), bf(4, 64, 512), bf(4, 64, 512),
            bf(2, 64, 512), bf(4, 64, 512), bf(4, 64, 512),
            bf(64, 512), pltpu.VMEM((512, 2048), F32), bf(512, 2048),
            pltpu.SemaphoreType.DMA((48,)), pltpu.SemaphoreType.DMA((48,)),
            pltpu.SemaphoreType.DMA((5,)), pltpu.SemaphoreType.DMA((4,)),
        ],
        compiler_params=pltpu.CompilerParams(
            collective_id=number, has_side_effects=True, vmem_limit_bytes=48 << 20
        ),
        name="gossip_steps",
    )(matching, weights, hidden, out_grad, factors)


def per_device(weights, hidden, out_grad, factor_start, matching):
    factors = factor_start.reshape(2 * RANK, factor_start.shape[2])
    return steps((None, None), 0, matching, weights, hidden, out_grad, factors)


def solution(mesh):
    return jax.shard_map(
        per_device,
        mesh=mesh,
        in_specs=(
            P("replica", "tensor", None),
            P("replica", None, "tensor"),
            P("replica", None, "tensor"),
            P(None, None, "tensor"),
            P(),
        ),
        out_specs=P("replica", "tensor", None),
        check_vma=False,
    )
```

time: 613 us -> 115 us (0.19)
  waiting for transfers between devices: 435 us -> 0 us
  Pallas kernels: 0 us -> 109 us
  starting transfers between devices: 95.5 us -> 0 us
  other arithmetic: 35.4 us -> 0 us
  between operations: 19 us -> 0.01 us
  matrix products: 18.9 us -> 0 us
    psum x2 -> x0, waiting for transfers between devices: 271 us -> none  [per_device(): lax.psum(local_left.astype(jnp.bfloat16), 'tensor').astype(jnp.float32)]
    pallas_call x0 -> x1, Pallas kernels: none -> 109 us  [steps(): pl.pallas_call(functools.partial(kernel, static), out_shape=jax.ShapeDtyp...]
    ppermute x20 -> x0, waiting for transfers between devices: 101 us -> none  [from_partner(): return lax.ppermute(value, axis, pairs)]
    ppermute x20 -> x0, starting transfers between devices: 95.4 us -> none  [from_partner(): return lax.ppermute(value, axis, pairs)]
    all_gather x2 -> x0, waiting for transfers between devices: 63.2 us -> none  [per_device(): lax.all_gather(grads_step, 'tensor', axis=1, tiled=True)]
    another operation x10 -> x0, other arithmetic: 24.8 us -> none  [the longest x6 13 us: orthonormal(): lower_factor = jnp.linalg.cholesky(gram_matrix)]
    dot_general x10 -> x0, matrix products: 16.9 us -> none  [the longest x2 5.15 us: per_device(): lax.dot_general(right_diff, ortho_bf, (((0,), (0,)), ((), ())), preferred...]
    convert_element_type x16 -> x0, other arithmetic: 10.6 us -> none  [the longest x8 10.5 us: swap_left_side(): payload.astype(jnp.bfloat16)]
  transfers between devices with their start and end apart: 24 -> 0, of which waited for: 21 -> 0; matrix products, arithmetic and copies ran while one was open for 3% -> 0% of each run, Pallas kernels for 0% -> 0%
where the time goes in v1:
time: 115 us
  Pallas kernels  109 us (95%)
  local copies, waits for them, and re-layouts  6.42 us (6%)
    pallas_call x1, Pallas kernels, steps(): pl.pallas_call(functools.partial(kernel, static), out_shape=jax.ShapeDtyp...  109 us
    unnamed x11, local copies, waits for them, and re-layouts  6.42 us

profile of v1, /device:TPU:1, one launch (start us, length us, event | category | flops | bytes accessed | tf_op | source)
XLA Modules:
  0.0 115.2 jit_solution(14556102853169323627)
XLA Ops:
  0.0 0.0 copy-start
  0.0 1.6 %copy-done = bf16[1,512,2048]{2,1,0:T(8,128)(2,1)S(1)} copy-done((bf16[1,512,2048]{2,1,0:T(8,128)(2,1)S(1)}, bf16[1,512,2048]{2,1,0:T(8,128)(2,1)}, u32[]{:S(2)}) %copy-start) | copy-done | bytes 2097176
  1.6 0.0 copy-start.1
  1.6 1.0 copy-done.1
  2.6 0.0 copy-start.2
  2.6 0.9 copy-done.2
  3.5 0.0 copy-start.3
  3.5 0.9 copy-done.3
  4.4 0.0 copy-start.4
  4.4 0.7 copy-done.4
  5.1 108.8 %gossip_steps.1 = bf16[1,512,2048]{2,1,0:T(8,128)(2,1)S(1)} custom-call(s32[2]{0:T(128)S(1)} %copy-done.4, bf16[1,512,2048]{2,1,0:T(8,128)(2,1)S(1)} %copy-done, bf16[1,512,512]{2,1,0:T(8,128)(2,1)S(1)} %copy-done.1, bf16[1,512,128]{2,1,0:T(8,128)(2,1)S(1)} %copy-done.2, bf16[128,512]{1,0:T(8,128)(2,1)S(1)} %bitcast.1), custom_call_target="tpu_custom_call" | custom-call | tf_op jit(solution)/shard_map/gossip_steps/pallas_call | solution.py:373
  113.9 1.3 %copy.7 = bf16[1,512,2048]{2,1,0:T(8,128)(2,1)} copy(bf16[1,512,2048]{2,1,0:T(8,128)(2,1)S(1)} %gossip_steps.1) | data formatting | bytes 4194304
Async XLA Ops:
  0.0 1.6 %copy-start = (bf16[1,512,2048]{2,1,0:T(8,128)(2,1)S(1)}, bf16[1,512,2048]{2,1,0:T(8,128)(2,1)}, u32[]{:S(2)}) copy-start(bf16[1,512,2048]{2,1,0:T(8,128)(2,1)} %w_hbm.1) | copy-start | bytes 6291460
  1.6 1.0 copy-start.1
  2.6 0.9 copy-start.2
  3.5 0.9 copy-start.3
  4.4 0.7 copy-start.4

commit v2 on v1

--- a/solution.py
+++ b/solution.py
@@ -71,11 +71,21 @@
     return wide[:, n:] * lax.rsqrt(pivots)
 
 
+def split(value):
+    high = value.astype(BF)
+    return high, (value - high.astype(F32)).astype(BF)
+
+
+def split_nn(a, b):
+    high, low = split(a)
+    if b.dtype == BF:
+        return nn(jnp.concatenate([high, low], axis=1), jnp.concatenate([b, b], axis=0))
+    b_high, b_low = split(b)
+    return nn(jnp.concatenate([high, low, high], axis=1), jnp.concatenate([b_high, b_high, b_low], axis=0))
+
+
 def orthonormal(diff):
-    inverse = inverse_lower_factor(nt(diff, diff))
-    high = inverse.astype(BF)
-    low = (inverse - high.astype(F32)).astype(BF)
-    return nn(jnp.concatenate([high, low], axis=1), jnp.concatenate([diff, diff], axis=0)).astype(BF)
+    return split_nn(inverse_lower_factor(nt(diff, diff)), diff).astype(BF)
 
 
 class Sends:
@@ -150,7 +160,7 @@
 def kernel(
     static, m_ref, w_hbm, h_hbm, g_hbm, s_hbm, o_hbm,
     w, h, s, gown, gf, tsend, trecv0, trecv1, tf, zsend, zrecv0, zrecv1, block,
-    c0, x0, z0, df0, ef, o0, cl, xl, zl, df1, o1, cr0, xr0, zr0, cr1, xr1, zr1,
+    c0, x0, z0, ce, xe, ze, df0, ef, o0, cl, xl, zl, df1, o1, cr0, xr0, zr0, cr1, xr1, zr1,
     rd0, v, out, send_sems, recv_sems, load_sems, store_sems,
 ):
     replica = lax.axis_index("replica")
@@ -193,9 +203,6 @@
         return carry
 
     lax.fori_loop(0, 4, starting_left, 0)
-    loads[3].wait()
-    loads[4].wait()
-
     pl.semaphore_wait(barrier, len(peers) + len(masks))
 
     sends = Sends(send_sems, recv_sems)
@@ -231,120 +238,155 @@
             total = total + arrived[k].astype(F32)
         return total
 
-    gshard = gown
-
-    def forward(dy_from, dz, dy_to):
-        cut = pl.ds(pl.multiple_of(at(dy_from, dz) * 128, 128), 128)
-        source = gown if (dy_from, dz) == (0, 0) else gf.at[:, cut]
-        return sends.start([(source, gf.at[:, cut], (replica, at(dy_to, 0)))], gshard)
+    ring = {}
+
+    def shard(dy, dz, to_dy, to_dz):
+        cut = pl.ds(pl.multiple_of(at(dy, dz) * 128, 128), 128)
+        source = gown if (dy, dz) == (0, 0) else gf.at[:, cut]
+        return sends.start([(source, gf.at[:, cut], (replica, at(to_dy, to_dz)))], gown)
+
+    def right(dy, dz):
+        ring[dy - 1, dz] = shard(dy, dz, 1, 0)
+
+    def left(dy, dz):
+        ring[dy + 1, dz] = shard(dy, dz, -1, 0)
+
+    def across(dy):
+        ring[dy, 1] = shard(dy, 0, 0, 1)
+
+    def arrived(dy, dz):
+        sends.wait(ring.pop((dy, dz)))
+
+    def pump0():
+        right(0, 0)
+        left(0, 0)
+        across(0)
+
+    def pump1():
+        arrived(-1, 0)
+        right(-1, 0)
+        arrived(1, 0)
+        left(1, 0)
+        across(-1)
+        across(1)
+
+    def pump2():
+        arrived(-2, 0)
+        right(-2, 0)
+        arrived(2, 0)
+        left(2, 0)
+        across(-2)
+        across(2)
+
+    def pump3():
+        arrived(-3, 0)
+        right(-3, 0)
+        arrived(-2, 1)
+        right(-2, 1)
+        arrived(2, 1)
+        left(2, 1)
+
+    def pump4():
+        arrived(3, 1)
+        left(3, 1)
+
+    def pump5():
+        for place in list(ring):
+            arrived(*place)
+
+    early = static[0] is not None
 
     t0 = scatter_tokens(0, trecv0)
     q0 = scatter_columns(0, zrecv0)
-    t1 = scatter_tokens(1, trecv1)
-    q1 = scatter_columns(1, zrecv1)
-    gz = sends.start([(gown, gf.at[:, mine], (replica, at(0, 1)))], gshard)
-    ra = forward(0, 0, 1)
-    la = forward(0, 0, -1)
-
     sends.wait(t0)
     t0 = sum_tokens(0, trecv0)
-    sends.wait(t1)
-    t1 = sum_tokens(1, trecv1)
+    q1 = scatter_columns(1, zrecv1)
+    t1 = scatter_tokens(1, trecv1)
+    loads[3].wait()
+    loads[4].wait()
+    pump0()
     sends.wait(q0)
     left0 = sum_columns(0, zrecv0)
-    sends.wait(q1)
-    left1 = sum_columns(1, zrecv1)
     sends.wait(t0)
     grad0 = tn(tf[pl.ds(0, TOK)], gown[pl.ds(0, TOK)])
     y0 = (left0 - 0.1 * grad0[:RANK]).astype(BF)
-    x1 = left1 - 0.1 * grad0[RANK:]
-
     first = Exchange(sends, replica, tensor, m_ref[0], static[0], (c0, x0, z0))
-    first.begin(jnp.concatenate([y0, x1.astype(BF)], axis=0))
-    sends.wait(gz)
-    rb = forward(0, 1, 1)
-    lb = forward(0, 1, -1)
+    cross = Exchange(sends, replica, tensor, m_ref[0], static[0], (ce, xe, ze))
+    first.begin(y0)
     first.along_x()
-    sends.wait(ra)
-    ra = forward(-1, 0, 1)
-    sends.wait(la)
-    la = forward(1, 0, -1)
+    sends.wait(q1)
+    x1 = sum_columns(1, zrecv1) - 0.1 * grad0[RANK:]
+    cross.begin(x1.astype(BF))
+    if early:
+        pump1()
+    sends.wait(t1)
+    t1 = sum_tokens(1, trecv1)
+    first.along_z()
+    cross.along_x()
+    if not early:
+        pump1()
+    diff = (y0.astype(F32) - first.end().astype(F32)).astype(BF)
+    block[0] = diff
+    df0[:, mine] = diff
+    d0 = gather_columns(block.at[0], df0)
+    cross.along_z()
+    both = (x1 + cross.end().astype(F32)).astype(BF)
+    block[1] = both
+    ef[:, mine] = both
+    e0 = gather_columns(block.at[1], ef)
+    pump2()
     sends.wait(t1)
     grad1 = tn(tf[pl.ds(TOK, TOK)], gown[pl.ds(TOK, TOK)])
     y1 = x1 - 0.09 * grad0[RANK:] - 0.1 * grad1[RANK:]
-    first.along_z()
-    sends.wait(rb)
-    rb = forward(-1, 1, 1)
-    sends.wait(lb)
-    lb = forward(1, 1, -1)
-    other = first.end()
-    diff = (y0.astype(F32) - other[:RANK].astype(F32)).astype(BF)
-    both = (x1 + other[RANK:].astype(F32)).astype(BF)
-    block[0] = diff
-    block[1] = both
-    df0[:, mine] = diff
-    ef[:, mine] = both
-    d0 = gather_columns(block.at[0], df0)
-    e0 = gather_columns(block.at[1], ef)
-    sends.wait(ra)
-    ra = forward(-2, 0, 1)
-    sends.wait(la)
-    la = forward(2, 0, -1)
     sends.wait(d0)
     o0[...] = orthonormal(df0[...])
+    if not early:
+        pump3()
     sends.wait(e0)
     moved = nt(ef[...], o0[...]).astype(BF)
     l1 = (y1 - 0.5 * nn(moved, o0[:, mine])).astype(BF)
-
     second = Exchange(sends, replica, tensor, m_ref[1], static[1], (cl, xl, zl))
     second.begin(l1)
-    sends.wait(rb)
-    rb = forward(-2, 1, 1)
-    sends.wait(lb)
-    lb = forward(2, 1, -1)
     second.along_x()
-    sends.wait(ra)
-    ra = forward(-3, 0, 1)
-    sends.wait(la)
-    sends.wait(rb)
-    sends.wait(lb)
-    lb = forward(3, 1, -1)
+    if early:
+        pump3()
     second.along_z()
-    sends.wait(ra)
-    sends.wait(lb)
+    pump4()
+    diff = (l1.astype(F32) - second.end().astype(F32)).astype(BF)
+    block[2] = diff
+    df1[:, mine] = diff
+    d1 = gather_columns(block.at[2], df1)
+    pump5()
     r0 = nt(o0[...], w[...]) - 0.1 * nn(nt(o0[...], gf[pl.ds(0, TOK)]).astype(BF), h[pl.ds(0, TOK)])
     r0 = r0.astype(BF)
     right0 = Exchange(sends, replica, tensor, m_ref[0], static[0], (cr0, xr0, zr0))
     right0.begin(r0)
-    diff = (l1.astype(F32) - second.end().astype(F32)).astype(BF)
-    block[2] = diff
-    df1[:, mine] = diff
-    d1 = gather_columns(block.at[2], df1)
     right0.along_x()
-    right0.along_z()
 
     def settled(i, carry):
         cut = pl.ds(pl.multiple_of(i * 256, 256), 256)
-        early = tn(h[pl.ds(0, TOK)], gf[pl.ds(0, TOK), cut])
-        late = tn(h[pl.ds(TOK, TOK)], gf[pl.ds(TOK, TOK), cut])
-        v[:, cut] = w[:, cut].astype(F32) - 0.19 * early - 0.1 * late
+        older = tn(h[pl.ds(0, TOK)], gf[pl.ds(0, TOK), cut])
+        newer = tn(h[pl.ds(TOK, TOK)], gf[pl.ds(TOK, TOK), cut])
+        v[:, cut] = w[:, cut].astype(F32) - 0.19 * older - 0.1 * newer
         return carry
 
+    lax.fori_loop(0, 8, settled, 0)
+    right0.along_z()
     sends.wait(d1)
-    o1[...] = orthonormal(df1[...])
-    grad_part = nt(o1[...], gf[...])
+    d1_all = df1[...]
+    grad_part = nt(d1_all, gf[...])
     grad_part = jnp.concatenate([0.19 * grad_part[:, :TOK], 0.1 * grad_part[:, TOK:]], axis=1).astype(BF)
-    cross = (0.5 * nt(o1[...], o0[...])).astype(BF)
-    r1 = nt(o1[...], w[...]) - nn(grad_part, h[...])
+    mixed = (0.5 * nt(d1_all, o0[...])).astype(BF)
+    k1 = nt(d1_all, w[...]) - nn(grad_part, h[...])
     diff0 = (r0.astype(F32) - right0.end().astype(F32)).astype(BF)
     rd0[...] = diff0
-    r1 = (r1 - nn(cross, diff0)).astype(BF)
+    k1 = (k1 - nn(mixed, diff0)).astype(BF)
     right1 = Exchange(sends, replica, tensor, m_ref[1], static[1], (cr1, xr1, zr1))
-    right1.begin(r1)
+    right1.begin(k1)
     right1.along_x()
-    lax.fori_loop(0, 4, settled, 0)
+    inverse = inverse_lower_factor(nt(d1_all, d1_all))
+    o1[...] = split_nn(inverse, d1_all).astype(BF)
     right1.along_z()
-    lax.fori_loop(4, 8, settled, 0)
 
     def first_move(i, carry):
         cut = pl.ds(pl.multiple_of(i * 256, 256), 256)
@@ -352,11 +394,12 @@
         return carry
 
     lax.fori_loop(0, 8, first_move, 0)
-    diff1 = (r1.astype(F32) - right1.end().astype(F32)).astype(BF)
+    apart = k1.astype(F32) - right1.end().astype(F32)
+    rd1 = split_nn(inverse, apart).astype(BF)
     stores = []
     for i in range(4):
         rows = pl.ds(128 * i, 128)
-        out[rows] = (v[rows] - 0.5 * tn(diff1[:, 128 * i : 128 * i + 128], o1[...])).astype(BF)
+        out[rows] = (v[rows] - 0.5 * tn(rd1[:, 128 * i : 128 * i + 128], o1[...])).astype(BF)
         store = pltpu.make_async_copy(out.at[rows], o_hbm.at[0, rows], store_sems.at[i])
         store.start()
         stores.append(store)
@@ -379,7 +422,8 @@
             bf(512, 2048), bf(512, 512), bf(128, 512), bf(512, 128), bf(512, 2048),
             bf(512, 128), bf(15, 16, 128), bf(15, 16, 128), bf(512, 128),
             bf(128, 2048), bf(15, 64, 128), bf(15, 64, 128), bf(3, 64, 128),
-            bf(2, 128, 128), bf(4, 128, 128), bf(4, 128, 128), bf(64, 2048), bf(64, 2048), bf(64, 2048),
+            bf(2, 64, 128), bf(4, 64, 128), bf(4, 64, 128), bf(2, 64, 128), bf(4, 64, 128), bf(4, 64, 128),
+            bf(64, 2048), bf(64, 2048), bf(64, 2048),
             bf(2, 64, 128), bf(4, 64, 128), bf(4, 64, 128), bf(64, 2048), bf(64, 2048),
             bf(2, 64, 512), bf(4, 64, 512), bf(4, 64, 512),
             bf(2, 64, 512), bf(4, 64, 512), bf(4, 64, 512),
@@ -388,7 +432,7 @@
             pltpu.SemaphoreType.DMA((5,)), pltpu.SemaphoreType.DMA((4,)),
         ],
         compiler_params=pltpu.CompilerParams(
-            collective_id=number, has_side_effects=True, vmem_limit_bytes=48 << 20
+            collective_id=number, has_side_effects=True, vmem_limit_bytes=60 << 20
         ),
         name="gossip_steps",
     )(matching, weights, hidden, out_grad, factors)
@@ -396,7 +440,12 @@
 
 def per_device(weights, hidden, out_grad, factor_start, matching):
     factors = factor_start.reshape(2 * RANK, factor_start.shape[2])
-    return steps((None, None), 0, matching, weights, hidden, out_grad, factors)
+    return lax.cond(
+        matching[0] == 31,
+        functools.partial(steps, (31, None), 0),
+        functools.partial(steps, (None, 31), 1),
+        matching, weights, hidden, out_grad, factors,
+    )
 
 
 def solution(mesh):

time: 115 us -> 95.7 us (0.83)
  Pallas kernels: 109 us -> 93.4 us
  local copies, waits for them, and re-layouts: 6.42 us -> 1.32 us
    pallas_call x1, Pallas kernels: 109 us -> 93.4 us  [steps(): pl.pallas_call(functools.partial(kernel, static), out_shape=jax.ShapeDtyp...]
    unnamed x11 -> x1, local copies, waits for them, and re-layouts: 6.42 us -> 1.32 us
where the time goes in v2:
time: 95.7 us; the launch traced here: 95.6 us
  Pallas kernels  93.4 us (98%)
  local copies, waits for them, and re-layouts  1.32 us (1%)
    pallas_call x1, Pallas kernels, steps(): pl.pallas_call(functools.partial(kernel, static), out_shape=jax.ShapeDtyp...  93.4 us

profile of v2, /device:TPU:1, one launch (start us, length us, event | category | flops | bytes accessed | tf_op | source)
XLA Modules:
  0.0 95.6 jit_solution(11227090279389287782)
XLA Ops:
  0.7 93.6 %conditional.1 = (bf16[1,512,2048]{2,1,0:T(8,128)(2,1)S(1)}) conditional(s32[]{:T(128)} %bitcast.2, (s32[2]{0:T(128)}, bf16[1,512,2048]{2,1,0:T(8,128)(2,1)}, bf16[1,512,512]{2,1,0:T(8,128)(2,1)}, bf16[1,512,128]{2,1,0:T(8,128)(2,1)}, bf16[2,64,512]{2,1,0:T(8,128)(2,1)}) %tuple.11, (s32[2]{0:T(128)}, bf16[1,512,2048]{2,1,0:T(8,128)(2,1)}, ...), branch_computations={%region_0.0_spmd, %region_1.0_spmd} | conditional | bytes 8 | solution.py:443
  0.9 93.4 %gossip_steps.3 = bf16[1,512,2048]{2,1,0:T(8,128)(2,1)S(1)} custom-call(s32[2]{0:T(128)} %get-tuple-element.33.m_ref, bf16[1,512,2048]{2,1,0:T(8,128)(2,1)} %get-tuple-element.48.w_hbm, bf16[1,512,512]{2,1,0:T(8,128)(2,1)} %get-tuple-element.50.h_hbm, bf16[1,512,128]{2,1,0:T(8,128)(2,1)} %get-tuple-element.52.g_hbm, bf16[128,512]{1,0:T(8,128)(2,1)} %bitcast.5), custom_call_target="tpu_custom_call" | custom-call | tf_op jit(solution)/shard_map/cond/branch_1_fun/gossip_steps/pallas_call | solution.py:416
  94.2 1.3 %copy.19 = bf16[1,512,2048]{2,1,0:T(8,128)(2,1)} copy(bf16[1,512,2048]{2,1,0:T(8,128)(2,1)S(1)} %get-tuple-element.38) | data formatting | bytes 4194304
